TPU v7x, 32 devices: a whole 2x2x4 slice. The times are simulated.
32 devices in a mesh: comp: 4 (over x, core), tile: 4 (over z), rep: 2 (over y).
Axes of the slice: x: 2, y: 2, z: 4, core: 2. Of those that a mesh axis runs over, the one named last changes fastest.
Arguments:
- retarded: bfloat16 [2, 16, 2, 192, 192], P(None, ('tile', 'rep')), may hold values from -0.3125 to 0.3125
- self_energy: bfloat16 [4, 16, 2, 192, 192], P('comp', ('tile', 'rep')), may hold values from -6 to 6
- energy_of: int32 [16], replicated, may hold values from 0 to 15, each once
Outputs:
- polar: float32 [4, 16, 2, 192, 192], P('comp', 'tile', None, 'rep')
Inputs may be any that keep to these rules, and one draw needn't show every extreme that they name: `energy_of`: each of the 16 energy grid indices stands in exactly one slot.
All inputs are finite; a program needn't handle non-finite values.
Results may differ from a plain program's by a relative error of at most 0.0095.
Values may be sent and summed in bfloat16 or wider, within the bound.
A program may use at most 64 MiB of HBM per device.

v0:
```python
import math

import jax
import jax.numpy as jnp
from jax import lax
from jax.sharding import PartitionSpec as P


def from_partner(array, axis, distance):
    return lax.ppermute(array, axis, [(i, i ^ 1 << distance) for i in range(lax.axis_size(axis))])


def batched(left_side, right_side, pattern):
    return jnp.einsum(pattern, left_side, right_side, preferred_element_type=jnp.float32)


def phase_tables(row_values, col_values, modulus):
    phase_index = row_values[:, None] * col_values[None, :] % modulus
    phase_angle = phase_index.astype(jnp.float32) * (2.0 * math.pi / modulus)
    cos_full = jnp.cos(phase_angle)
    sin_full = jnp.sin(phase_angle)
    cos_high = cos_full.astype(jnp.bfloat16)
    sin_high = sin_full.astype(jnp.bfloat16)
    cos_low = (cos_full - cos_high.astype(jnp.float32)).astype(jnp.bfloat16)
    sin_low = (sin_full - sin_high.astype(jnp.float32)).astype(jnp.bfloat16)
    return ((cos_high, cos_low), (sin_high, sin_low))


def split_dot(table_pair, values):
    return jnp.dot(table_pair[0], values, preferred_element_type=jnp.float32) + jnp.dot(
        table_pair[1], values, preferred_element_type=jnp.float32
    )


def rotate(cos_table, sin_table, value_re, value_im, direction):
    part_re = split_dot(cos_table, value_re) - direction * split_dot(sin_table, value_im)
    part_im = split_dot(cos_table, value_im) + direction * split_dot(sin_table, value_re)
    return (part_re, part_im)


def body(retarded, self_energy, energy_of):
    component = lax.axis_index("comp")
    momentum = component // 2
    greater = component % 2
    tile_count = lax.axis_size("tile")
    rep_count = lax.axis_size("rep")
    green_matrix = lax.dynamic_index_in_dim(retarded, momentum, 0, keepdims=False)
    sigma_matrix = self_energy[0]
    green_re, green_im = (green_matrix[:, 0], green_matrix[:, 1])
    sigma_re, sigma_im = (sigma_matrix[:, 0], sigma_matrix[:, 1])
    left_re = (
        batched(green_re, sigma_re, "eik,ekj->eij") - batched(green_im, sigma_im, "eik,ekj->eij")
    ).astype(jnp.bfloat16)
    left_im = (
        batched(green_re, sigma_im, "eik,ekj->eij") + batched(green_im, sigma_re, "eik,ekj->eij")
    ).astype(jnp.bfloat16)
    out_re = batched(left_re, green_re, "eik,ejk->eij") + batched(left_im, green_im, "eik,ejk->eij")
    out_im = batched(left_im, green_re, "eik,ejk->eij") - batched(left_re, green_im, "eik,ejk->eij")
    stacked = jnp.stack([out_re, out_im]).astype(jnp.bfloat16)
    stacked = jnp.where(greater == 1, jnp.swapaxes(stacked, 2, 3), stacked)
    energy_dev = stacked.shape[1]
    block_order = stacked.shape[2]
    elem_count = block_order * block_order // (tile_count * rep_count)
    slot_count = energy_of.shape[0]
    blocks = stacked.reshape(2, energy_dev, rep_count, tile_count, elem_count)
    first_pass = lax.all_to_all(blocks, "rep", split_axis=2, concat_axis=1, tiled=True)
    gathered = lax.all_to_all(first_pass, "tile", split_axis=3, concat_axis=1, tiled=True)
    signal = gathered.reshape(2, slot_count, elem_count)
    freq_count = 2 * slot_count
    frequency = lax.iota(jnp.int32, freq_count)
    fwd_cos, fwd_sin = phase_tables(frequency, energy_of, freq_count)
    own_re, own_im = rotate(fwd_cos, fwd_sin, signal[0], signal[1], -1.0)
    partner = from_partner(signal, "comp", 0)
    other_re, other_im = rotate(fwd_cos, fwd_sin, partner[0], partner[1], 1.0)
    cross_re = (own_re * other_re - own_im * other_im).astype(jnp.bfloat16)
    cross_im = (own_re * other_im + own_im * other_re).astype(jnp.bfloat16)
    lag_index = lax.iota(jnp.int32, slot_count)
    inv_cos, inv_sin = phase_tables(lag_index, frequency, freq_count)
    back_re, back_im = rotate(inv_cos, inv_sin, cross_re, cross_im, 1.0)
    norm_factor = 1.0 / (freq_count * math.sqrt(slot_count))
    polar_parts = jnp.stack([back_im * norm_factor, -back_re * norm_factor], axis=1)
    regrouped = lax.all_to_all(
        polar_parts[:, :, None, :], "tile", split_axis=0, concat_axis=2, tiled=True
    )
    lag_count = slot_count // tile_count
    return regrouped.reshape(lag_count, 2, block_order // rep_count, block_order)[None]


def solution(mesh):
    placed = (
        P(None, ("tile", "rep"), None, None, None),
        P("comp", ("tile", "rep"), None, None, None),
        P(),
    )
    return jax.shard_map(
        body,
        mesh=mesh,
        in_specs=placed,
        out_specs=P("comp", "tile", None, "rep", None),
        check_vma=False,
    )
```

profile of v0, /device:TPU:0, one launch (start us, length us, event | category | flops | bytes accessed | tf_op | source)
XLA Modules:
  0.0 57.4 jit_solution(12100221358946152259)
XLA Ops:
  0.0 1.1 %copy-done = bf16[2,2,2,192,192]{4,3,2,1,0:T(8,128)(2,1)S(1)} copy-done((bf16[2,2,2,192,192]{4,3,2,1,0:T(8,128)(2,1)S(1)}, bf16[2,2,2,192,192]{4,3,2,1,0:T(8,128)(2,1)}, u32[]{:S(2)}) %copy-start) | copy-done | bytes 589848
  1.1 1.0 %copy_bitcast_fusion = (bf16[2,2,192,192]{3,2,0,1:T(8,128)(2,1)S(1)}, bf16[2,2,192,192]{3,2,0,1:T(8,128)(2,1)S(1)}) fusion(bf16[1,2,2,192,192]{4,3,2,1,0:T(8,128)(2,1)} %param.4, bf16[2,2,2,192,192]{4,3,2,1,0:T(8,128)(2,1)S(1)} %copy-done, s32[]{:T(128)S(6)} %select_n.54), kind=kLoop, calls=%fused_computation.40 | loop fusion | bytes 1277956 | tf_op jit(solution)/shard_map/squeeze | solution.py:48
  4.4 0.4 reshape.13
  4.9 9.6 %all_to_all.48 = bf16[2,2,2,4,4608]{4,3,1,0,2:T(4,128)(2,1)S(1)} all-to-all(bf16[2,2,2,4,4608]{4,3,1,0,2:T(4,128)(2,1)S(1)} %copy.27), channel_id=1, replica_groups=mesh['comp'=4,'tile'=4,'rep'=2] {'rep'}, dimensions={2} | all-to-all | bytes 589824 | tf_op jit(solution)/shard_map/all_to_all | solution.py:66
  14.6 13.2 %all_to_all.49 = bf16[2,4,1,4,4608]{4,1,0,2,3:T(4,128)(2,1)S(1)} all-to-all(bf16[2,4,1,4,4608]{4,1,0,2,3:T(4,128)(2,1)S(1)} %copy.29), channel_id=1, replica_groups=mesh['comp'=4,'tile'=4,'rep'=2] {'tile'}, dimensions={3} | all-to-all | bytes 589824 | tf_op jit(solution)/shard_map/all_to_all | solution.py:67
  28.2 0.6 %copy-done.1 = s32[16]{0:T(128)S(1)} copy-done((s32[16]{0:T(128)S(1)}, s32[16]{0:T(128)}, u32[]{:S(2)}) %copy-start.1) | copy-done | bytes 88
  29.1 0.3 fusion.49
  29.8 0.3 fusion.1
  30.1 0.3 fusion.4
  30.4 0.3 fusion
  31.0 0.3 fusion.3
  31.3 0.4 fusion.171
  31.7 0.3 fusion.27
  32.0 0.3 fusion.30
  32.3 0.3 fusion.24
  32.6 0.3 fusion.21
  32.9 0.3 convolution_add_fusion
  33.2 0.3 convolution_add_fusion.4
  33.5 0.3 fusion.2
  33.7 0.4 add_convert_fusion
  36.0 0.5 copy.31
  36.5 19.2 %all_to_all.50 = f32[16,2,1,4608]{3,1,2,0:T(2,128)S(1)} all-to-all(f32[16,2,1,4608]{3,1,2,0:T(2,128)S(1)} %copy.31), channel_id=1, replica_groups=mesh['comp'=4,'tile'=4,'rep'=2] {'tile'}, dimensions={0} | all-to-all | bytes 1179648 | tf_op jit(solution)/shard_map/all_to_all | solution.py:82
  55.7 0.4 copy.32
  56.1 1.3 %broadcast_in_dim_reshape.3 = f32[1,4,2,96,192]{4,3,2,1,0:T(8,128)} reshape(f32[4,2,4,1,4608]{4,2,1,0,3:T(4,128)S(1)} %copy.32) | data formatting | bytes 1179648 | tf_op jit(solution)/shard_map/broadcast_in_dim;reshape | solution.py:86
  (36 shorter events, 5.6 us)
Async XLA Ops:
  0.0 1.1 %copy-start = (bf16[2,2,2,192,192]{4,3,2,1,0:T(8,128)(2,1)S(1)}, bf16[2,2,2,192,192]{4,3,2,1,0:T(8,128)(2,1)}, u32[]{:S(2)}) copy-start(bf16[2,2,2,192,192]{4,3,2,1,0:T(8,128)(2,1)} %param.3) | copy-start | bytes 1769476
  28.2 0.7 %copy-start.1 = (s32[16]{0:T(128)S(1)}, s32[16]{0:T(128)}, u32[]{:S(2)}) copy-start(s32[16]{0:T(128)} %param.5) | copy-start | bytes 196
  29.4 1.9 %collective-permute-start = (bf16[2,16,4608]{2,0,1:T(2,128)(2,1)S(1)}, bf16[2,16,4608]{2,0,1:T(2,128)(2,1)S(1)}, u32[]{:S(2)}, u32[]{:S(2)}) collective-permute-start(bf16[2,16,4608]{2,0,1:T(2,128)(2,1)S(1)} %bitcast.100), channel_id=1, source_target_pairs={{0,8},{8,0},{16,24},{24,16},{1,9},{9,1},{17,25},{25,17},{2,10},{10... | collective-permute-start | bytes 884744 | tf_op jit(solution)/shard_map/ppermute | solution.py:10
where the time goes:
time: 57.7 us; the launch traced here: 57.4 us
  blocking collectives  42 us (73%)
  matrix products  8.16 us (14%)
  local copies, waits for them, and re-layouts  6.64 us (12%)
    all_to_all x1, blocking collectives, body(): lax.all_to_all(polar_parts[:, :, None, :], 'tile', split_axis=0, concat_a...  19.2 us
    all_to_all x1, blocking collectives, body(): lax.all_to_all(first_pass, 'tile', split_axis=3, concat_axis=1, tiled=True)  13.2 us
    all_to_all x1, blocking collectives, body(): lax.all_to_all(blocks, 'rep', split_axis=2, concat_axis=1, tiled=True)  9.55 us
    dot_general x12, matrix products, split_dot(): jnp.dot(table_pair[0], values, preferred_element_type=jnp.float32)  3.22 us
    dot_general x12, matrix products, split_dot(): jnp.dot(table_pair[1], values, preferred_element_type=jnp.float32)  3.21 us
    unnamed x6, local copies, waits for them, and re-layouts  1.78 us
    dot_general x8, matrix products, batched(): jnp.einsum(pattern, left_side, right_side, preferred_element_type=jnp.flo...  1.73 us
    another operation x1, local copies, waits for them, and re-layouts, body(): regrouped.reshape(lag_count, 2, block_order // rep_count, block_order)[None]  1.26 us
  transfers between devices with their start and end apart: 1, of which 0 were waited for; matrix products, arithmetic and copies ran while one was open for 3% of the time, Pallas kernels for 0%

commit v1 on v0

--- a/solution.py
+++ b/solution.py
@@ -1,8 +1,11 @@
+import functools
 import math
 
 import jax
 import jax.numpy as jnp
 from jax import lax
+from jax.experimental import pallas as pl
+from jax.experimental.pallas import tpu as pltpu
 from jax.sharding import PartitionSpec as P
 
 
@@ -86,14 +89,329 @@
     return regrouped.reshape(lag_count, 2, block_order // rep_count, block_order)[None]
 
 
+LANES = 128
+ROWS = 8
+
+
+def matmul(left_side, right_side, contract):
+    return lax.dot_general(
+        left_side, right_side, (((1,), (contract,)), ((), ())), preferred_element_type=jnp.float32
+    )
+
+
+def rotated(values):
+    return pltpu.roll(values, LANES // 2, axis=1)
+
+
+def polar_kernel(
+    axis_sizes,
+    retarded,
+    self_energy,
+    energy_of,
+    polar,
+    green_in,
+    sigma_in,
+    energies,
+    outgoing,
+    ordered,
+    lagged,
+    arrived,
+    load_sem,
+    first_send,
+    first_recv,
+    second_send,
+    second_recv,
+    *gathered,
+):
+    tile_count, rep_count = axis_sizes
+    component = lax.axis_index("comp")
+    tile = lax.axis_index("tile")
+    rep = lax.axis_index("rep")
+    momentum = component // 2
+    greater = component % 2
+    energy_dev, block_order = green_in.shape[0], green_in.shape[2]
+    slot_count = energies.shape[0]
+    unit_count = arrived.shape[0]
+    lag_count = arrived.shape[1]
+    row_count = block_order // rep_count
+    low_units = row_count // ROWS
+    owner_count = 2 * tile_count
+    peer_count = owner_count * rep_count
+    base_units = unit_count // owner_count
+    has_spare = unit_count % owner_count != 0
+
+    place = (tile * 2 + greater) * rep_count + rep
+    owner = tile * 2 + greater
+
+    def first_unit(which):
+        return which * unit_count // owner_count
+
+    def takes_spare(which):
+        return first_unit(which + 1) - first_unit(which) > base_units
+
+    def device_of(which_owner, which_rep):
+        return (momentum * 2 + which_owner % 2, which_owner // 2, which_rep)
+
+    loads = []
+    for energy in range(energy_dev):
+        loads.append(
+            (
+                pltpu.make_async_copy(
+                    retarded.at[momentum, energy], green_in.at[energy], load_sem.at[2 * energy]
+                ),
+                pltpu.make_async_copy(
+                    self_energy.at[0, energy], sigma_in.at[energy], load_sem.at[2 * energy + 1]
+                ),
+            )
+        )
+        for load in loads[-1]:
+            load.start()
+    energy_load = pltpu.make_async_copy(energy_of, energies, load_sem.at[2 * energy_dev])
+    energy_load.start()
+
+    barrier = pltpu.get_barrier_semaphore()
+    for step in range(1, peer_count):
+        peer = (place + step) % peer_count
+        pl.semaphore_signal(
+            barrier,
+            inc=1,
+            device_id=device_of(peer // rep_count, peer % rep_count),
+            device_id_type=pl.DeviceIdType.MESH,
+        )
+
+    def finish(energy, left, right, sign):
+        low, high = slice(0, LANES), slice(LANES, block_order)
+        right_re, right_im = right
+        with_re = jnp.concatenate(
+            [right_re[low], -sign * right_im[low], right_re[high], -sign * right_im[high]]
+        )
+        with_im = jnp.concatenate(
+            [right_im[low], sign * right_re[low], right_im[high], sign * right_re[high]]
+        )
+        result = matmul(left[0], with_re, 1) + matmul(left[1], with_im, 1)
+        is_low = lax.broadcasted_iota(jnp.int32, (row_count // 2, LANES), 1) < LANES // 2
+        for part in range(rep_count):
+            rows = slice(part * row_count, (part + 1) * row_count)
+            mixed = result[rows, 2 * LANES :]
+            upper, lower = mixed[: row_count // 2], mixed[row_count // 2 :]
+            high_re = jnp.where(is_low, upper, rotated(lower))
+            high_im = jnp.where(is_low, rotated(upper), lower)
+            pieces_re = jnp.concatenate([result[rows, :LANES], high_re])
+            pieces_im = jnp.concatenate([result[rows, LANES : 2 * LANES], high_im])
+            packed = jnp.concatenate(
+                [
+                    pieces_re.reshape(unit_count, ROWS, LANES),
+                    pieces_im.reshape(unit_count, ROWS, LANES),
+                ],
+                axis=1,
+            )
+            outgoing[part, :, energy] = packed.astype(jnp.bfloat16)
+
+    for energy in range(energy_dev):
+        for load in loads[energy]:
+            load.wait()
+        green_re, green_im = green_in[energy, 0], green_in[energy, 1]
+        sigma_re, sigma_im = sigma_in[energy, 0], sigma_in[energy, 1]
+        left_re = (matmul(green_re, sigma_re, 0) - matmul(green_im, sigma_im, 0)).astype(jnp.bfloat16)
+        left_im = (matmul(green_re, sigma_im, 0) + matmul(green_im, sigma_re, 0)).astype(jnp.bfloat16)
+
+        @pl.when(greater == 0)
+        def _():
+            finish(energy, (left_re, left_im), (green_re, green_im), 1)
+
+        @pl.when(greater == 1)
+        def _():
+            finish(energy, (green_re, green_im), (left_re, left_im), -1)
+
+    pl.semaphore_wait(barrier, peer_count - 1)
+
+    my_slot = greater * slot_count + (tile * rep_count + rep) * energy_dev
+
+    def send_first(unit, spare):
+        for step in range(1, peer_count):
+            peer = (place + step) % peer_count
+            peer_owner, peer_rep = peer // rep_count, peer % rep_count
+            copy = pltpu.make_async_remote_copy(
+                src_ref=outgoing.at[peer_rep, first_unit(peer_owner) + unit],
+                dst_ref=gathered[unit].at[pl.ds(my_slot, energy_dev)],
+                send_sem=first_send.at[unit],
+                recv_sem=first_recv.at[unit],
+                device_id=device_of(peer_owner, peer_rep),
+                device_id_type=pl.DeviceIdType.MESH,
+            )
+            if spare:
+                pl.when(takes_spare(peer_owner))(copy.start)
+            else:
+                copy.start()
+
+    def keep_own(unit):
+        gathered[unit][pl.ds(my_slot, energy_dev)] = outgoing[rep, first_unit(owner) + unit]
+
+    def wait_for(buffer, sem):
+        pltpu.make_async_copy(buffer, buffer, sem).wait()
+
+    for unit in range(base_units):
+        send_first(unit, False)
+    if has_spare:
+        send_first(base_units, True)
+    for unit in range(base_units):
+        keep_own(unit)
+    if has_spare:
+        pl.when(takes_spare(owner))(functools.partial(keep_own, base_units))
+
+    energy_load.wait()
+    slots = []
+    for energy in range(slot_count):
+        slot = 0
+        for candidate in range(slot_count):
+            slot = jnp.where(energies[candidate] == energy, candidate, slot)
+        slots.append(slot)
+
+    norm_factor = 1.0 / math.sqrt(slot_count)
+
+    def correlate(unit):
+        wait_for(
+            gathered[unit].at[pl.ds(0, (peer_count - 1) * energy_dev)], first_recv.at[unit]
+        )
+        for part in range(2):
+            for energy in range(slot_count):
+                ordered[part, energy] = gathered[unit][part * slot_count + slots[energy]].astype(
+                    jnp.float32
+                )
+        for lag in range(slot_count):
+            for part in range(2):
+                own_re = ordered[part, lag:, :ROWS]
+                own_im = ordered[part, lag:, ROWS:]
+                other_re = ordered[1 - part, : slot_count - lag, :ROWS]
+                other_im = ordered[1 - part, : slot_count - lag, ROWS:]
+                sum_re = jnp.sum(own_re * other_re - own_im * other_im, axis=0)
+                sum_im = jnp.sum(own_re * other_im + own_im * other_re, axis=0)
+                lagged[unit, part, lag] = jnp.concatenate(
+                    [sum_im * norm_factor, sum_re * -norm_factor]
+                ).astype(jnp.bfloat16)
+        my_unit = first_unit(owner) + unit
+        for step in range(1, owner_count):
+            peer = (owner + step) % owner_count
+            pltpu.make_async_remote_copy(
+                src_ref=lagged.at[unit, peer % 2, pl.ds(peer // 2 * lag_count, lag_count)],
+                dst_ref=arrived.at[my_unit],
+                send_sem=second_send.at[unit],
+                recv_sem=second_recv.at[unit],
+                device_id=device_of(peer, rep),
+                device_id_type=pl.DeviceIdType.MESH,
+            ).start()
+        arrived[my_unit] = lagged[unit, greater, pl.ds(tile * lag_count, lag_count)]
+
+    for unit in range(base_units):
+        correlate(unit)
+    if has_spare:
+        pl.when(takes_spare(owner))(functools.partial(correlate, base_units))
+
+    for unit in range(base_units):
+        wait_for(
+            gathered[unit].at[pl.ds(0, (peer_count - 1) * energy_dev)], first_send.at[unit]
+        )
+        wait_for(arrived.at[pl.ds(0, owner_count - 1)], second_send.at[unit])
+        wait_for(arrived.at[pl.ds(0, owner_count - 1)], second_recv.at[unit])
+    if has_spare:
+        spare_units = unit_count % owner_count
+        spares = spare_units * rep_count
+
+        @pl.when(takes_spare(owner))
+        def _():
+            if spares > 1:
+                wait_for(
+                    gathered[base_units].at[pl.ds(0, (spares - 1) * energy_dev)],
+                    first_send.at[base_units],
+                )
+            wait_for(arrived.at[pl.ds(0, owner_count - 1)], second_send.at[base_units])
+            if spare_units > 1:
+                wait_for(arrived.at[pl.ds(0, spare_units - 1)], second_recv.at[base_units])
+
+        @pl.when(jnp.logical_not(takes_spare(owner)))
+        def _():
+            wait_for(
+                gathered[base_units].at[pl.ds(0, spares * energy_dev)], first_send.at[base_units]
+            )
+            wait_for(arrived.at[pl.ds(0, spare_units)], second_recv.at[base_units])
+
+    for lag in range(lag_count):
+        for unit in range(unit_count):
+            values = arrived[unit, lag].astype(jnp.float32)
+            for part in range(2):
+                block = values[part * ROWS : (part + 1) * ROWS]
+                if unit < low_units:
+                    polar[0, lag, part, unit * ROWS : (unit + 1) * ROWS, :LANES] = block
+                else:
+                    row = (unit - low_units) * ROWS
+                    row_low = row + row_count // 2
+                    polar[0, lag, part, row : row + ROWS, LANES:] = block[:, : LANES // 2]
+                    polar[0, lag, part, row_low : row_low + ROWS, LANES:] = rotated(block)[
+                        :, : LANES // 2
+                    ]
+
+
+def fits(sizes, energy_dev, block_order):
+    comp_count, tile_count, rep_count = sizes
+    return (
+        comp_count % 2 == 0
+        and block_order == LANES + LANES // 2
+        and block_order % (2 * ROWS * 2 * rep_count) == 0
+        and block_order * 3 // (4 * ROWS * rep_count) >= 2 * tile_count
+        and tile_count * rep_count * energy_dev <= 4 * ROWS
+    )
+
+
+def fused(sizes, retarded, self_energy, energy_of):
+    _, tile_count, rep_count = sizes
+    energy_dev, block_order = retarded.shape[1], retarded.shape[-1]
+    slot_count = energy_of.shape[0]
+    lag_count = slot_count // tile_count
+    row_count = block_order // rep_count
+    unit_count = row_count * block_order // (ROWS * LANES)
+    units_held = -(-unit_count // (2 * tile_count))
+    packed = (2 * ROWS, LANES)
+    return pl.pallas_call(
+        functools.partial(polar_kernel, (tile_count, rep_count)),
+        out_shape=jax.ShapeDtypeStruct((1, lag_count, 2, row_count, block_order), jnp.float32),
+        in_specs=[pl.BlockSpec(memory_space=pl.ANY)] * 3,
+        out_specs=pl.BlockSpec(memory_space=pltpu.VMEM),
+        scratch_shapes=[
+            pltpu.VMEM(retarded.shape[1:], jnp.bfloat16),
+            pltpu.VMEM(self_energy.shape[1:], jnp.bfloat16),
+            pltpu.SMEM((slot_count,), jnp.int32),
+            pltpu.VMEM((rep_count, unit_count, energy_dev) + packed, jnp.bfloat16),
+            pltpu.VMEM((2, slot_count) + packed, jnp.float32),
+            pltpu.VMEM((units_held, 2, slot_count) + packed, jnp.bfloat16),
+            pltpu.VMEM((unit_count, lag_count) + packed, jnp.bfloat16),
+            pltpu.SemaphoreType.DMA((2 * energy_dev + 1,)),
+            pltpu.SemaphoreType.DMA((units_held,)),
+            pltpu.SemaphoreType.DMA((units_held,)),
+            pltpu.SemaphoreType.DMA((units_held,)),
+            pltpu.SemaphoreType.DMA((units_held,)),
+        ]
+        + [pltpu.VMEM((2 * slot_count,) + packed, jnp.bfloat16)] * units_held,
+        compiler_params=pltpu.CompilerParams(
+            collective_id=0, has_side_effects=True, vmem_limit_bytes=40 * 2**20
+        ),
+    )(retarded, self_energy, energy_of)
+
+
 def solution(mesh):
     placed = (
         P(None, ("tile", "rep"), None, None, None),
         P("comp", ("tile", "rep"), None, None, None),
         P(),
     )
+    sizes = tuple(mesh.shape[name] for name in ("comp", "tile", "rep"))
+
+    def device_body(retarded, self_energy, energy_of):
+        if fits(sizes, retarded.shape[1], retarded.shape[-1]):
+            return fused(sizes, retarded, self_energy, energy_of)
+        return body(retarded, self_energy, energy_of)
+
     return jax.shard_map(
-        body,
+        device_body,
         mesh=mesh,
         in_specs=placed,
         out_specs=P("comp", "tile", None, "rep", None),

time: 57.7 us -> 24.4 us (0.42)
  blocking collectives: 42 us -> 0 us
  Pallas kernels: 0 us -> 20.5 us
  matrix products: 8.16 us -> 0 us
  local copies, waits for them, and re-layouts: 6.64 us -> 3.66 us
    all_to_all x3 -> x0, blocking collectives: 42 us -> none  [the longest x1 19.2 us: body(): lax.all_to_all(polar_parts[:, :, None, :], 'tile', split_axis=0, concat_a...]
    pallas_call x0 -> x1, Pallas kernels: none -> 20.5 us  [fused(): pl.pallas_call(functools.partial(polar_kernel, (tile_count, rep_count)),...]
    dot_general x32 -> x0, matrix products: 8.16 us -> none  [the longest x12 3.22 us: split_dot(): jnp.dot(table_pair[0], values, preferred_element_type=jnp.float32)]
    unnamed x6 -> x7, local copies, waits for them, and re-layouts: 1.78 us -> 3.66 us
    another operation x2 -> x0, local copies, waits for them, and re-layouts: 1.46 us -> none  [the longest x1 1.26 us: body(): regrouped.reshape(lag_count, 2, block_order // rep_count, block_order)[None]]
    squeeze x3 -> x0, local copies, waits for them, and re-layouts: 1.13 us -> none  [the longest x1 1.05 us: body(): sigma_matrix = self_energy[0]]
    all_to_all x4 -> x0, local copies, waits for them, and re-layouts: 0.83 us -> none  [the longest x1 0.38 us: body(): lax.all_to_all(polar_parts[:, :, None, :], 'tile', split_axis=0, concat_a...]
  transfers between devices with their start and end apart: 1 -> 0, of which waited for: 0 -> 0; matrix products, arithmetic and copies ran while one was open for 3% -> 0% of each run, Pallas kernels for 0% -> 0%
where the time goes in v1:
time: 24.4 us; the launch traced here: 24.2 us
  Pallas kernels  20.5 us (84%)
  local copies, waits for them, and re-layouts  3.66 us (15%)
    pallas_call x1, Pallas kernels, fused(): pl.pallas_call(functools.partial(polar_kernel, (tile_count, rep_count)),...  20.5 us
    unnamed x7, local copies, waits for them, and re-layouts  3.66 us

profile of v1, /device:TPU:0, one launch (start us, length us, event | category | flops | bytes accessed | tf_op | source)
XLA Modules:
  0.0 24.2 jit_solution(574011193993372403)
XLA Ops:
  0.0 0.0 copy-start
  0.0 1.1 %copy-done = bf16[2,2,2,192,192]{4,3,2,1,0:T(8,128)(2,1)S(1)} copy-done((bf16[2,2,2,192,192]{4,3,2,1,0:T(8,128)(2,1)S(1)}, bf16[2,2,2,192,192]{4,3,2,1,0:T(8,128)(2,1)}, u32[]{:S(2)}) %copy-start) | copy-done | bytes 589848
  1.1 0.0 copy-start.1
  1.1 1.0 %copy-done.1 = bf16[1,2,2,192,192]{4,3,2,1,0:T(8,128)(2,1)S(1)} copy-done((bf16[1,2,2,192,192]{4,3,2,1,0:T(8,128)(2,1)S(1)}, bf16[1,2,2,192,192]{4,3,2,1,0:T(8,128)(2,1)}, u32[]{:S(2)}) %copy-start.1) | copy-done | bytes 294936
  2.1 0.0 copy-start.2
  2.1 0.7 %copy-done.2 = s32[16]{0:T(128)S(1)} copy-done((s32[16]{0:T(128)S(1)}, s32[16]{0:T(128)}, u32[]{:S(2)}) %copy-start.2) | copy-done | bytes 88
  2.8 20.5 %shard_map.37 = f32[1,4,2,96,192]{4,3,2,1,0:T(8,128)S(1)} custom-call(bf16[2,2,2,192,192]{4,3,2,1,0:T(8,128)(2,1)S(1)} %copy-done, bf16[1,2,2,192,192]{4,3,2,1,0:T(8,128)(2,1)S(1)} %copy-done.1, s32[16]{0:T(128)S(1)} %copy-done.2), custom_call_target="tpu_custom_call" | custom-call | tf_op jit(solution)/shard_map/pallas_call | solution.py:374
  23.3 0.9 %copy.5 = f32[1,4,2,96,192]{4,3,2,1,0:T(8,128)} copy(f32[1,4,2,96,192]{4,3,2,1,0:T(8,128)S(1)} %shard_map.37) | data formatting | bytes 1179648
Async XLA Ops:
  0.0 1.1 %copy-start = (bf16[2,2,2,192,192]{4,3,2,1,0:T(8,128)(2,1)S(1)}, bf16[2,2,2,192,192]{4,3,2,1,0:T(8,128)(2,1)}, u32[]{:S(2)}) copy-start(bf16[2,2,2,192,192]{4,3,2,1,0:T(8,128)(2,1)} %retarded.1) | copy-start | bytes 1769476
  1.1 1.0 %copy-start.1 = (bf16[1,2,2,192,192]{4,3,2,1,0:T(8,128)(2,1)S(1)}, bf16[1,2,2,192,192]{4,3,2,1,0:T(8,128)(2,1)}, u32[]{:S(2)}) copy-start(bf16[1,2,2,192,192]{4,3,2,1,0:T(8,128)(2,1)} %self_energy.1) | copy-start | bytes 884740
  2.1 0.7 %copy-start.2 = (s32[16]{0:T(128)S(1)}, s32[16]{0:T(128)}, u32[]{:S(2)}) copy-start(s32[16]{0:T(128)} %energy_of.1) | copy-start | bytes 196

commit v2 on v1

--- a/solution.py
+++ b/solution.py
@@ -140,7 +140,6 @@
     base_units = unit_count // owner_count
     has_spare = unit_count % owner_count != 0
 
-    place = (tile * 2 + greater) * rep_count + rep
     owner = tile * 2 + greater
 
     def first_unit(which):
@@ -149,8 +148,24 @@
     def takes_spare(which):
         return first_unit(which + 1) - first_unit(which) > base_units
 
-    def device_of(which_owner, which_rep):
-        return (momentum * 2 + which_owner % 2, which_owner // 2, which_rep)
+    tiles = [(tile + step) % tile_count for step in range(tile_count)]
+    reps = [(rep + step) % rep_count for step in range(rep_count)]
+    parts = [greater, 1 - greater]
+    owners = [[tiles[i] * 2 + parts[j] for j in range(2)] for i in range(tile_count)]
+    firsts = [[first_unit(owners[i][j]) for j in range(2)] for i in range(tile_count)]
+    spares_at = [[takes_spare(owners[i][j]) for j in range(2)] for i in range(tile_count)]
+    far_first = sorted(range(tile_count), key=lambda step: -min(step, tile_count - step))
+    near_owners = [(i, j) for j in range(2) for i in far_first if (i, j) != (0, 0)]
+    peers = [
+        (i, j, k)
+        for k in reversed(range(rep_count))
+        for j in range(2)
+        for i in far_first
+        if (i, j, k) != (0, 0, 0)
+    ]
+
+    def device_of(i, j, k):
+        return (momentum * 2 + parts[j], tiles[i], reps[k])
 
     loads = []
     for energy in range(energy_dev):
@@ -170,12 +185,11 @@
     energy_load.start()
 
     barrier = pltpu.get_barrier_semaphore()
-    for step in range(1, peer_count):
-        peer = (place + step) % peer_count
+    for peer in peers:
         pl.semaphore_signal(
             barrier,
             inc=1,
-            device_id=device_of(peer // rep_count, peer % rep_count),
+            device_id=device_of(*peer),
             device_id_type=pl.DeviceIdType.MESH,
         )
 
@@ -228,24 +242,22 @@
     my_slot = greater * slot_count + (tile * rep_count + rep) * energy_dev
 
     def send_first(unit, spare):
-        for step in range(1, peer_count):
-            peer = (place + step) % peer_count
-            peer_owner, peer_rep = peer // rep_count, peer % rep_count
+        for i, j, k in peers:
             copy = pltpu.make_async_remote_copy(
-                src_ref=outgoing.at[peer_rep, first_unit(peer_owner) + unit],
+                src_ref=outgoing.at[reps[k], firsts[i][j] + unit],
                 dst_ref=gathered[unit].at[pl.ds(my_slot, energy_dev)],
                 send_sem=first_send.at[unit],
                 recv_sem=first_recv.at[unit],
-                device_id=device_of(peer_owner, peer_rep),
+                device_id=device_of(i, j, k),
                 device_id_type=pl.DeviceIdType.MESH,
             )
             if spare:
-                pl.when(takes_spare(peer_owner))(copy.start)
+                pl.when(spares_at[i][j])(copy.start)
             else:
                 copy.start()
 
     def keep_own(unit):
-        gathered[unit][pl.ds(my_slot, energy_dev)] = outgoing[rep, first_unit(owner) + unit]
+        gathered[unit][pl.ds(my_slot, energy_dev)] = outgoing[rep, firsts[0][0] + unit]
 
     def wait_for(buffer, sem):
         pltpu.make_async_copy(buffer, buffer, sem).wait()
@@ -257,7 +269,7 @@
     for unit in range(base_units):
         keep_own(unit)
     if has_spare:
-        pl.when(takes_spare(owner))(functools.partial(keep_own, base_units))
+        pl.when(spares_at[0][0])(functools.partial(keep_own, base_units))
 
     energy_load.wait()
     slots = []
@@ -289,15 +301,14 @@
                 lagged[unit, part, lag] = jnp.concatenate(
                     [sum_im * norm_factor, sum_re * -norm_factor]
                 ).astype(jnp.bfloat16)
-        my_unit = first_unit(owner) + unit
-        for step in range(1, owner_count):
-            peer = (owner + step) % owner_count
+        my_unit = firsts[0][0] + unit
+        for i, j in near_owners:
             pltpu.make_async_remote_copy(
-                src_ref=lagged.at[unit, peer % 2, pl.ds(peer // 2 * lag_count, lag_count)],
+                src_ref=lagged.at[unit, parts[j], pl.ds(tiles[i] * lag_count, lag_count)],
                 dst_ref=arrived.at[my_unit],
                 send_sem=second_send.at[unit],
                 recv_sem=second_recv.at[unit],
-                device_id=device_of(peer, rep),
+                device_id=device_of(i, j, 0),
                 device_id_type=pl.DeviceIdType.MESH,
             ).start()
         arrived[my_unit] = lagged[unit, greater, pl.ds(tile * lag_count, lag_count)]
@@ -305,7 +316,7 @@
     for unit in range(base_units):
         correlate(unit)
     if has_spare:
-        pl.when(takes_spare(owner))(functools.partial(correlate, base_units))
+        pl.when(spares_at[0][0])(functools.partial(correlate, base_units))
 
     for unit in range(base_units):
         wait_for(
@@ -317,7 +328,7 @@
         spare_units = unit_count % owner_count
         spares = spare_units * rep_count
 
-        @pl.when(takes_spare(owner))
+        @pl.when(spares_at[0][0])
         def _():
             if spares > 1:
                 wait_for(
@@ -328,7 +339,7 @@
             if spare_units > 1:
                 wait_for(arrived.at[pl.ds(0, spare_units - 1)], second_recv.at[base_units])
 
-        @pl.when(jnp.logical_not(takes_spare(owner)))
+        @pl.when(jnp.logical_not(spares_at[0][0]))
         def _():
             wait_for(
                 gathered[base_units].at[pl.ds(0, spares * energy_dev)], first_send.at[base_units]
@@ -392,7 +403,7 @@
         ]
         + [pltpu.VMEM((2 * slot_count,) + packed, jnp.bfloat16)] * units_held,
         compiler_params=pltpu.CompilerParams(
-            collective_id=0, has_side_effects=True, vmem_limit_bytes=40 * 2**20
+            collective_id=0, has_side_effects=True, vmem_limit_bytes=62 * 2**20
         ),
     )(retarded, self_energy, energy_of)
 

time: 24.4 us -> 23.5 us (0.963)
  local copies, waits for them, and re-layouts: 3.66 us -> 2.06 us
  Pallas kernels: 20.5 us -> 21.3 us
    unnamed x7 -> x1, local copies, waits for them, and re-layouts: 3.66 us -> 2.06 us
    pallas_call x1, Pallas kernels: 20.5 us -> 21.3 us  [fused(): pl.pallas_call(functools.partial(polar_kernel, (tile_count, rep_count)),...]
where the time goes in v2:
time: 23.5 us; the launch traced here: 23.3 us
  Pallas kernels  21.3 us (91%)
  local copies, waits for them, and re-layouts  2.06 us (9%)
    pallas_call x1, Pallas kernels, fused(): pl.pallas_call(functools.partial(polar_kernel, (tile_count, rep_count)),...  21.3 us
    unnamed x1, local copies, waits for them, and re-layouts  2.06 us

profile of v2, /device:TPU:0, one launch (start us, length us, event | category | flops | bytes accessed | tf_op | source)
XLA Modules:
  0.0 23.3 jit_solution(4494238479803795716)
XLA Ops:
  0.0 21.3 %shard_map.37 = f32[1,4,2,96,192]{4,3,2,1,0:T(8,128)} custom-call(bf16[2,2,2,192,192]{4,3,2,1,0:T(8,128)(2,1)} %retarded.1, bf16[1,2,2,192,192]{4,3,2,1,0:T(8,128)(2,1)} %self_energy.1, s32[16]{0:T(128)} %energy_of.1), custom_call_target="tpu_custom_call" | custom-call | tf_op jit(solution)/shard_map/pallas_call | solution.py:385
  21.3 2.1 %copy.5 = f32[1,4,2,96,192]{4,3,2,1,0:T(8,128)} copy(f32[1,4,2,96,192]{4,3,2,1,0:T(8,128)} %shard_map.37) | data formatting | bytes 1179648

commit v3 on v2

--- a/solution.py
+++ b/solution.py
@@ -91,6 +91,7 @@
 
 LANES = 128
 ROWS = 8
+KERNEL_BYTES = 62 * 2**20
 
 
 def matmul(left_side, right_side, contract):
@@ -108,19 +109,19 @@
     retarded,
     self_energy,
     energy_of,
-    polar,
+    arrived,
     green_in,
     sigma_in,
     energies,
     outgoing,
     ordered,
     lagged,
-    arrived,
     load_sem,
     first_send,
     first_recv,
     second_send,
     second_recv,
+    keep_sem,
     *gathered,
 ):
     tile_count, rep_count = axis_sizes
@@ -280,6 +281,13 @@
         slots.append(slot)
 
     norm_factor = 1.0 / math.sqrt(slot_count)
+
+    def keep_lags(unit):
+        return pltpu.make_async_copy(
+            lagged.at[unit, greater, pl.ds(tile * lag_count, lag_count)],
+            arrived.at[firsts[0][0] + unit],
+            keep_sem.at[unit],
+        )
 
     def correlate(unit):
         wait_for(
@@ -311,7 +319,7 @@
                 device_id=device_of(i, j, 0),
                 device_id_type=pl.DeviceIdType.MESH,
             ).start()
-        arrived[my_unit] = lagged[unit, greater, pl.ds(tile * lag_count, lag_count)]
+        keep_lags(unit).start()
 
     for unit in range(base_units):
         correlate(unit)
@@ -324,6 +332,7 @@
         )
         wait_for(arrived.at[pl.ds(0, owner_count - 1)], second_send.at[unit])
         wait_for(arrived.at[pl.ds(0, owner_count - 1)], second_recv.at[unit])
+        keep_lags(unit).wait()
     if has_spare:
         spare_units = unit_count % owner_count
         spares = spare_units * rep_count
@@ -336,6 +345,7 @@
                     first_send.at[base_units],
                 )
             wait_for(arrived.at[pl.ds(0, owner_count - 1)], second_send.at[base_units])
+            keep_lags(base_units).wait()
             if spare_units > 1:
                 wait_for(arrived.at[pl.ds(0, spare_units - 1)], second_recv.at[base_units])
 
@@ -346,20 +356,39 @@
             )
             wait_for(arrived.at[pl.ds(0, spare_units)], second_recv.at[base_units])
 
+
+def unpack_kernel(arrived, polar, packed, unpacked, load_sem, store_sem):
+    unit_count, lag_count = arrived.shape[:2]
+    row_count = polar.shape[3]
+    low_units = row_count // ROWS
+    loads = [
+        pltpu.make_async_copy(arrived.at[:, lag], packed.at[lag], load_sem.at[lag])
+        for lag in range(lag_count)
+    ]
+    stores = [
+        pltpu.make_async_copy(unpacked.at[lag], polar.at[0, lag], store_sem.at[lag])
+        for lag in range(lag_count)
+    ]
+    for load in loads:
+        load.start()
     for lag in range(lag_count):
+        loads[lag].wait()
         for unit in range(unit_count):
-            values = arrived[unit, lag].astype(jnp.float32)
+            values = packed[lag, unit].astype(jnp.float32)
             for part in range(2):
                 block = values[part * ROWS : (part + 1) * ROWS]
                 if unit < low_units:
-                    polar[0, lag, part, unit * ROWS : (unit + 1) * ROWS, :LANES] = block
+                    unpacked[lag, part, unit * ROWS : (unit + 1) * ROWS, :LANES] = block
                 else:
                     row = (unit - low_units) * ROWS
                     row_low = row + row_count // 2
-                    polar[0, lag, part, row : row + ROWS, LANES:] = block[:, : LANES // 2]
-                    polar[0, lag, part, row_low : row_low + ROWS, LANES:] = rotated(block)[
+                    unpacked[lag, part, row : row + ROWS, LANES:] = block[:, : LANES // 2]
+                    unpacked[lag, part, row_low : row_low + ROWS, LANES:] = rotated(block)[
                         :, : LANES // 2
                     ]
+        stores[lag].start()
+    for store in stores:
+        store.wait()
 
 
 def fits(sizes, energy_dev, block_order):
@@ -382,11 +411,11 @@
     unit_count = row_count * block_order // (ROWS * LANES)
     units_held = -(-unit_count // (2 * tile_count))
     packed = (2 * ROWS, LANES)
-    return pl.pallas_call(
+    arrived = pl.pallas_call(
         functools.partial(polar_kernel, (tile_count, rep_count)),
-        out_shape=jax.ShapeDtypeStruct((1, lag_count, 2, row_count, block_order), jnp.float32),
+        out_shape=jax.ShapeDtypeStruct((unit_count, lag_count) + packed, jnp.bfloat16),
         in_specs=[pl.BlockSpec(memory_space=pl.ANY)] * 3,
-        out_specs=pl.BlockSpec(memory_space=pltpu.VMEM),
+        out_specs=pl.BlockSpec(memory_space=pl.ANY),
         scratch_shapes=[
             pltpu.VMEM(retarded.shape[1:], jnp.bfloat16),
             pltpu.VMEM(self_energy.shape[1:], jnp.bfloat16),
@@ -394,8 +423,8 @@
             pltpu.VMEM((rep_count, unit_count, energy_dev) + packed, jnp.bfloat16),
             pltpu.VMEM((2, slot_count) + packed, jnp.float32),
             pltpu.VMEM((units_held, 2, slot_count) + packed, jnp.bfloat16),
-            pltpu.VMEM((unit_count, lag_count) + packed, jnp.bfloat16),
             pltpu.SemaphoreType.DMA((2 * energy_dev + 1,)),
+            pltpu.SemaphoreType.DMA((units_held,)),
             pltpu.SemaphoreType.DMA((units_held,)),
             pltpu.SemaphoreType.DMA((units_held,)),
             pltpu.SemaphoreType.DMA((units_held,)),
@@ -403,9 +432,22 @@
         ]
         + [pltpu.VMEM((2 * slot_count,) + packed, jnp.bfloat16)] * units_held,
         compiler_params=pltpu.CompilerParams(
-            collective_id=0, has_side_effects=True, vmem_limit_bytes=62 * 2**20
+            collective_id=0, has_side_effects=True, vmem_limit_bytes=KERNEL_BYTES
         ),
     )(retarded, self_energy, energy_of)
+    return pl.pallas_call(
+        unpack_kernel,
+        out_shape=jax.ShapeDtypeStruct((1, lag_count, 2, row_count, block_order), jnp.float32),
+        in_specs=[pl.BlockSpec(memory_space=pl.ANY)],
+        out_specs=pl.BlockSpec(memory_space=pl.ANY),
+        scratch_shapes=[
+            pltpu.VMEM((lag_count, unit_count) + packed, jnp.bfloat16),
+            pltpu.VMEM((lag_count, 2, row_count, block_order), jnp.float32),
+            pltpu.SemaphoreType.DMA((lag_count,)),
+            pltpu.SemaphoreType.DMA((lag_count,)),
+        ],
+        compiler_params=pltpu.CompilerParams(vmem_limit_bytes=KERNEL_BYTES),
+    )(arrived)
 
 
 def solution(mesh):

time: 23.5 us -> 22.5 us (0.957)
  local copies, waits for them, and re-layouts: 2.06 us -> 0 us
  Pallas kernels: 21.3 us -> 22.4 us
    unnamed x1 -> x0, local copies, waits for them, and re-layouts: 2.06 us -> none
    pallas_call x0 -> x1, Pallas kernels: none -> 1.94 us  [fused(): pl.pallas_call(unpack_kernel, out_shape=jax.ShapeDtypeStruct((1, lag_coun...]
    pallas_call x1, Pallas kernels: 21.3 us -> 20.4 us  [fused(): pl.pallas_call(functools.partial(polar_kernel, (tile_count, rep_count)),...]
where the time goes in v3:
time: 22.5 us; the launch traced here: 22.4 us
  Pallas kernels  22.4 us (100%)
    pallas_call x1, Pallas kernels, fused(): pl.pallas_call(functools.partial(polar_kernel, (tile_count, rep_count)),...  20.4 us
    pallas_call x1, Pallas kernels, fused(): pl.pallas_call(unpack_kernel, out_shape=jax.ShapeDtypeStruct((1, lag_coun...  1.94 us

profile of v3, /device:TPU:0, one launch (start us, length us, event | category | flops | bytes accessed | tf_op | source)
XLA Modules:
  0.0 22.4 jit_solution(1233340155079552433)
XLA Ops:
  0.0 20.4 %shard_map.37.arrived = bf16[18,4,16,128]{3,2,1,0:T(8,128)(2,1)} custom-call(bf16[2,2,2,192,192]{4,3,2,1,0:T(8,128)(2,1)} %retarded.1, bf16[1,2,2,192,192]{4,3,2,1,0:T(8,128)(2,1)} %self_energy.1, s32[16]{0:T(128)} %energy_of.1), custom_call_target="tpu_custom_call" | custom-call | tf_op jit(solution)/shard_map/pallas_call | solution.py:414
  20.4 1.9 %shard_map.38 = f32[1,4,2,96,192]{4,3,2,1,0:T(8,128)} custom-call(bf16[18,4,16,128]{3,2,1,0:T(8,128)(2,1)} %shard_map.37.arrived), custom_call_target="tpu_custom_call" | custom-call | tf_op jit(solution)/shard_map/pallas_call | solution.py:438

commit v4 on v3

--- a/solution.py
+++ b/solution.py
@@ -149,19 +149,26 @@
     def takes_spare(which):
         return first_unit(which + 1) - first_unit(which) > base_units
 
-    tiles = [(tile + step) % tile_count for step in range(tile_count)]
+    half = tile_count // 2
+    if tile_count % 2 == 0:
+        own_half = tile // half * half
+        other_half = (own_half + half) % tile_count
+        tiles = [own_half + (tile + step) % half for step in range(half)]
+        tiles += [other_half + (tile + step) % half for step in range(half)]
+    else:
+        tiles = [(tile + step) % tile_count for step in range(tile_count)]
     reps = [(rep + step) % rep_count for step in range(rep_count)]
     parts = [greater, 1 - greater]
     owners = [[tiles[i] * 2 + parts[j] for j in range(2)] for i in range(tile_count)]
     firsts = [[first_unit(owners[i][j]) for j in range(2)] for i in range(tile_count)]
     spares_at = [[takes_spare(owners[i][j]) for j in range(2)] for i in range(tile_count)]
-    far_first = sorted(range(tile_count), key=lambda step: -min(step, tile_count - step))
-    near_owners = [(i, j) for j in range(2) for i in far_first if (i, j) != (0, 0)]
+    far_first = [(step + half) % tile_count for step in range(tile_count)]
+    near_owners = [(i, j) for i in far_first for j in range(2) if (i, j) != (0, 0)]
     peers = [
         (i, j, k)
+        for i in far_first
         for k in reversed(range(rep_count))
         for j in range(2)
-        for i in far_first
         if (i, j, k) != (0, 0, 0)
     ]
 
@@ -222,6 +229,26 @@
             )
             outgoing[part, :, energy] = packed.astype(jnp.bfloat16)
 
+    my_slot = greater * slot_count + (tile * rep_count + rep) * energy_dev
+
+    def send_first(unit, energy):
+        for i, j, k in peers:
+            copy = pltpu.make_async_remote_copy(
+                src_ref=outgoing.at[reps[k], firsts[i][j] + unit, energy],
+                dst_ref=gathered[unit].at[my_slot + energy],
+                send_sem=first_send.at[unit],
+                recv_sem=first_recv.at[unit],
+                device_id=device_of(i, j, k),
+                device_id_type=pl.DeviceIdType.MESH,
+            )
+            if unit < base_units:
+                copy.start()
+            else:
+                pl.when(spares_at[i][j])(copy.start)
+
+    def keep_own(unit):
+        gathered[unit][pl.ds(my_slot, energy_dev)] = outgoing[rep, firsts[0][0] + unit]
+
     for energy in range(energy_dev):
         for load in loads[energy]:
             load.wait()
@@ -238,35 +265,14 @@
         def _():
             finish(energy, (green_re, green_im), (left_re, left_im), -1)
 
-    pl.semaphore_wait(barrier, peer_count - 1)
-
-    my_slot = greater * slot_count + (tile * rep_count + rep) * energy_dev
-
-    def send_first(unit, spare):
-        for i, j, k in peers:
-            copy = pltpu.make_async_remote_copy(
-                src_ref=outgoing.at[reps[k], firsts[i][j] + unit],
-                dst_ref=gathered[unit].at[pl.ds(my_slot, energy_dev)],
-                send_sem=first_send.at[unit],
-                recv_sem=first_recv.at[unit],
-                device_id=device_of(i, j, k),
-                device_id_type=pl.DeviceIdType.MESH,
-            )
-            if spare:
-                pl.when(spares_at[i][j])(copy.start)
-            else:
-                copy.start()
-
-    def keep_own(unit):
-        gathered[unit][pl.ds(my_slot, energy_dev)] = outgoing[rep, firsts[0][0] + unit]
+        if energy == 0:
+            pl.semaphore_wait(barrier, peer_count - 1)
+        for unit in range(base_units + has_spare):
+            send_first(unit, energy)
 
     def wait_for(buffer, sem):
         pltpu.make_async_copy(buffer, buffer, sem).wait()
 
-    for unit in range(base_units):
-        send_first(unit, False)
-    if has_spare:
-        send_first(base_units, True)
     for unit in range(base_units):
         keep_own(unit)
     if has_spare:

time: 22.5 us -> 24.3 us (1.080)
  Pallas kernels: 22.4 us -> 24.1 us
    pallas_call x1, Pallas kernels: 20.4 us -> 22.2 us  [fused(): pl.pallas_call(functools.partial(polar_kernel, (tile_count, rep_count)),...]
where the time goes in v4:
time: 24.3 us; the launch traced here: 24.2 us
  Pallas kernels  24.1 us (99%)
    pallas_call x1, Pallas kernels, fused(): pl.pallas_call(functools.partial(polar_kernel, (tile_count, rep_count)),...  22.2 us
    pallas_call x1, Pallas kernels, fused(): pl.pallas_call(unpack_kernel, out_shape=jax.ShapeDtypeStruct((1, lag_coun...  1.94 us

profile of v4, /device:TPU:0, one launch (start us, length us, event | category | flops | bytes accessed | tf_op | source)
XLA Modules:
  0.0 24.2 jit_solution(4929892077139782521)
XLA Ops:
  0.0 22.2 %shard_map.37.arrived = bf16[18,4,16,128]{3,2,1,0:T(8,128)(2,1)} custom-call(bf16[2,2,2,192,192]{4,3,2,1,0:T(8,128)(2,1)} %retarded.1, bf16[1,2,2,192,192]{4,3,2,1,0:T(8,128)(2,1)} %self_energy.1, s32[16]{0:T(128)} %energy_of.1), custom_call_target="tpu_custom_call" | custom-call | tf_op jit(solution)/shard_map/pallas_call | solution.py:420
  22.2 1.9 %shard_map.38 = f32[1,4,2,96,192]{4,3,2,1,0:T(8,128)} custom-call(bf16[18,4,16,128]{3,2,1,0:T(8,128)(2,1)} %shard_map.37.arrived), custom_call_target="tpu_custom_call" | custom-call | tf_op jit(solution)/shard_map/pallas_call | solution.py:444

commit v5 on v4

--- a/solution.py
+++ b/solution.py
@@ -231,11 +231,11 @@
 
     my_slot = greater * slot_count + (tile * rep_count + rep) * energy_dev
 
-    def send_first(unit, energy):
+    def send_first(unit):
         for i, j, k in peers:
             copy = pltpu.make_async_remote_copy(
-                src_ref=outgoing.at[reps[k], firsts[i][j] + unit, energy],
-                dst_ref=gathered[unit].at[my_slot + energy],
+                src_ref=outgoing.at[reps[k], firsts[i][j] + unit],
+                dst_ref=gathered[unit].at[pl.ds(my_slot, energy_dev)],
                 send_sem=first_send.at[unit],
                 recv_sem=first_recv.at[unit],
                 device_id=device_of(i, j, k),
@@ -265,10 +265,9 @@
         def _():
             finish(energy, (green_re, green_im), (left_re, left_im), -1)
 
-        if energy == 0:
-            pl.semaphore_wait(barrier, peer_count - 1)
-        for unit in range(base_units + has_spare):
-            send_first(unit, energy)
+    pl.semaphore_wait(barrier, peer_count - 1)
+    for unit in range(base_units + has_spare):
+        send_first(unit)
 
     def wait_for(buffer, sem):
         pltpu.make_async_copy(buffer, buffer, sem).wait()

time: 24.3 us -> 22.5 us (0.926)
  Pallas kernels: 24.1 us -> 22.3 us
    pallas_call x1, Pallas kernels: 22.2 us -> 20.4 us  [fused(): pl.pallas_call(functools.partial(polar_kernel, (tile_count, rep_count)),...]
where the time goes in v5:
time: 22.5 us; the launch traced here: 22.3 us
  Pallas kernels  22.3 us (99%)
    pallas_call x1, Pallas kernels, fused(): pl.pallas_call(functools.partial(polar_kernel, (tile_count, rep_count)),...  20.4 us
    pallas_call x1, Pallas kernels, fused(): pl.pallas_call(unpack_kernel, out_shape=jax.ShapeDtypeStruct((1, lag_coun...  1.94 us

profile of v5, /device:TPU:0, one launch (start us, length us, event | category | flops | bytes accessed | tf_op | source)
XLA Modules:
  0.0 22.3 jit_solution(3082837216996573376)
XLA Ops:
  0.0 20.4 %shard_map.37.arrived = bf16[18,4,16,128]{3,2,1,0:T(8,128)(2,1)} custom-call(bf16[2,2,2,192,192]{4,3,2,1,0:T(8,128)(2,1)} %retarded.1, bf16[1,2,2,192,192]{4,3,2,1,0:T(8,128)(2,1)} %self_energy.1, s32[16]{0:T(128)} %energy_of.1), custom_call_target="tpu_custom_call" | custom-call | tf_op jit(solution)/shard_map/pallas_call | solution.py:419
  20.4 1.9 %shard_map.38 = f32[1,4,2,96,192]{4,3,2,1,0:T(8,128)} custom-call(bf16[18,4,16,128]{3,2,1,0:T(8,128)(2,1)} %shard_map.37.arrived), custom_call_target="tpu_custom_call" | custom-call | tf_op jit(solution)/shard_map/pallas_call | solution.py:443

commit v6 on v5

--- a/solution.py
+++ b/solution.py
@@ -229,25 +229,29 @@
             )
             outgoing[part, :, energy] = packed.astype(jnp.bfloat16)
 
-    my_slot = greater * slot_count + (tile * rep_count + rep) * energy_dev
-
-    def send_first(unit):
+    half_count = tile_count * rep_count
+    my_place = greater * half_count + tile * rep_count + rep
+    groups = [(0, base_units)] + [(base_units, 1)] * has_spare
+
+    def send_first(group):
+        start, size = groups[group]
         for i, j, k in peers:
             copy = pltpu.make_async_remote_copy(
-                src_ref=outgoing.at[reps[k], firsts[i][j] + unit],
-                dst_ref=gathered[unit].at[pl.ds(my_slot, energy_dev)],
-                send_sem=first_send.at[unit],
-                recv_sem=first_recv.at[unit],
+                src_ref=outgoing.at[reps[k], pl.ds(firsts[i][j] + start, size)],
+                dst_ref=gathered[group].at[my_place],
+                send_sem=first_send.at[group],
+                recv_sem=first_recv.at[group],
                 device_id=device_of(i, j, k),
                 device_id_type=pl.DeviceIdType.MESH,
             )
-            if unit < base_units:
+            if start == 0:
                 copy.start()
             else:
                 pl.when(spares_at[i][j])(copy.start)
 
-    def keep_own(unit):
-        gathered[unit][pl.ds(my_slot, energy_dev)] = outgoing[rep, firsts[0][0] + unit]
+    def keep_own(group):
+        start, size = groups[group]
+        gathered[group][my_place] = outgoing[rep, pl.ds(firsts[0][0] + start, size)]
 
     for energy in range(energy_dev):
         for load in loads[energy]:
@@ -266,24 +270,25 @@
             finish(energy, (green_re, green_im), (left_re, left_im), -1)
 
     pl.semaphore_wait(barrier, peer_count - 1)
-    for unit in range(base_units + has_spare):
-        send_first(unit)
+    for group in range(len(groups)):
+        send_first(group)
 
     def wait_for(buffer, sem):
         pltpu.make_async_copy(buffer, buffer, sem).wait()
 
-    for unit in range(base_units):
-        keep_own(unit)
+    keep_own(0)
     if has_spare:
-        pl.when(spares_at[0][0])(functools.partial(keep_own, base_units))
+        pl.when(spares_at[0][0])(functools.partial(keep_own, 1))
 
     energy_load.wait()
     slots = []
     for energy in range(slot_count):
-        slot = 0
+        source, local = 0, 0
         for candidate in range(slot_count):
-            slot = jnp.where(energies[candidate] == energy, candidate, slot)
-        slots.append(slot)
+            held = energies[candidate] == energy
+            source = jnp.where(held, candidate // energy_dev, source)
+            local = jnp.where(held, candidate % energy_dev, local)
+        slots.append((source, local))
 
     norm_factor = 1.0 / math.sqrt(slot_count)
 
@@ -295,14 +300,15 @@
         )
 
     def correlate(unit):
-        wait_for(
-            gathered[unit].at[pl.ds(0, (peer_count - 1) * energy_dev)], first_recv.at[unit]
-        )
+        group = unit // base_units
+        start, _ = groups[group]
+        if unit == start:
+            wait_for(gathered[group].at[pl.ds(0, peer_count - 1)], first_recv.at[group])
         for part in range(2):
-            for energy in range(slot_count):
-                ordered[part, energy] = gathered[unit][part * slot_count + slots[energy]].astype(
-                    jnp.float32
-                )
+            for energy, (source, local) in enumerate(slots):
+                ordered[part, energy] = gathered[group][
+                    part * half_count + source, unit - start, local
+                ].astype(jnp.float32)
         for lag in range(slot_count):
             for part in range(2):
                 own_re = ordered[part, lag:, :ROWS]
@@ -331,10 +337,8 @@
     if has_spare:
         pl.when(spares_at[0][0])(functools.partial(correlate, base_units))
 
+    wait_for(gathered[0].at[pl.ds(0, peer_count - 1)], first_send.at[0])
     for unit in range(base_units):
-        wait_for(
-            gathered[unit].at[pl.ds(0, (peer_count - 1) * energy_dev)], first_send.at[unit]
-        )
         wait_for(arrived.at[pl.ds(0, owner_count - 1)], second_send.at[unit])
         wait_for(arrived.at[pl.ds(0, owner_count - 1)], second_recv.at[unit])
         keep_lags(unit).wait()
@@ -345,10 +349,7 @@
         @pl.when(spares_at[0][0])
         def _():
             if spares > 1:
-                wait_for(
-                    gathered[base_units].at[pl.ds(0, (spares - 1) * energy_dev)],
-                    first_send.at[base_units],
-                )
+                wait_for(gathered[1].at[pl.ds(0, spares - 1)], first_send.at[1])
             wait_for(arrived.at[pl.ds(0, owner_count - 1)], second_send.at[base_units])
             keep_lags(base_units).wait()
             if spare_units > 1:
@@ -356,9 +357,7 @@
 
         @pl.when(jnp.logical_not(spares_at[0][0]))
         def _():
-            wait_for(
-                gathered[base_units].at[pl.ds(0, spares * energy_dev)], first_send.at[base_units]
-            )
+            wait_for(gathered[1].at[pl.ds(0, spares)], first_send.at[1])
             wait_for(arrived.at[pl.ds(0, spare_units)], second_recv.at[base_units])
 
 
@@ -414,7 +413,9 @@
     lag_count = slot_count // tile_count
     row_count = block_order // rep_count
     unit_count = row_count * block_order // (ROWS * LANES)
+    base_units = unit_count // (2 * tile_count)
     units_held = -(-unit_count // (2 * tile_count))
+    group_sizes = [base_units] + [1] * (units_held - base_units)
     packed = (2 * ROWS, LANES)
     arrived = pl.pallas_call(
         functools.partial(polar_kernel, (tile_count, rep_count)),
@@ -435,7 +436,10 @@
             pltpu.SemaphoreType.DMA((units_held,)),
             pltpu.SemaphoreType.DMA((units_held,)),
         ]
-        + [pltpu.VMEM((2 * slot_count,) + packed, jnp.bfloat16)] * units_held,
+        + [
+            pltpu.VMEM((2 * tile_count * rep_count, size, energy_dev) + packed, jnp.bfloat16)
+            for size in group_sizes
+        ],
         compiler_params=pltpu.CompilerParams(
             collective_id=0, has_side_effects=True, vmem_limit_bytes=KERNEL_BYTES
         ),

time: 22.5 us -> 23.5 us (1.044)
  Pallas kernels: 22.3 us -> 23.3 us
    pallas_call x1, Pallas kernels: 20.4 us -> 21.4 us  [fused(): pl.pallas_call(functools.partial(polar_kernel, (tile_count, rep_count)),...]
where the time goes in v6:
time: 23.5 us; the launch traced here: 23.3 us
  Pallas kernels  23.3 us (99%)
    pallas_call x1, Pallas kernels, fused(): pl.pallas_call(functools.partial(polar_kernel, (tile_count, rep_count)),...  21.4 us
    pallas_call x1, Pallas kernels, fused(): pl.pallas_call(unpack_kernel, out_shape=jax.ShapeDtypeStruct((1, lag_coun...  1.94 us

profile of v6, /device:TPU:0, one launch (start us, length us, event | category | flops | bytes accessed | tf_op | source)
XLA Modules:
  0.0 23.3 jit_solution(7465436216988281313)
XLA Ops:
  0.0 21.4 %shard_map.37.arrived = bf16[18,4,16,128]{3,2,1,0:T(8,128)(2,1)} custom-call(bf16[2,2,2,192,192]{4,3,2,1,0:T(8,128)(2,1)} %retarded.1, bf16[1,2,2,192,192]{4,3,2,1,0:T(8,128)(2,1)} %self_energy.1, s32[16]{0:T(128)} %energy_of.1), custom_call_target="tpu_custom_call" | custom-call | tf_op jit(solution)/shard_map/pallas_call | solution.py:420
  21.4 1.9 %shard_map.38 = f32[1,4,2,96,192]{4,3,2,1,0:T(8,128)} custom-call(bf16[18,4,16,128]{3,2,1,0:T(8,128)(2,1)} %shard_map.37.arrived), custom_call_target="tpu_custom_call" | custom-call | tf_op jit(solution)/shard_map/pallas_call | solution.py:447

commit v7 on v5

--- a/solution.py
+++ b/solution.py
@@ -163,7 +163,6 @@
     firsts = [[first_unit(owners[i][j]) for j in range(2)] for i in range(tile_count)]
     spares_at = [[takes_spare(owners[i][j]) for j in range(2)] for i in range(tile_count)]
     far_first = [(step + half) % tile_count for step in range(tile_count)]
-    near_owners = [(i, j) for i in far_first for j in range(2) if (i, j) != (0, 0)]
     peers = [
         (i, j, k)
         for i in far_first
@@ -249,6 +248,7 @@
     def keep_own(unit):
         gathered[unit][pl.ds(my_slot, energy_dev)] = outgoing[rep, firsts[0][0] + unit]
 
+    greens, lefts = [], []
     for energy in range(energy_dev):
         for load in loads[energy]:
             load.wait()
@@ -256,14 +256,18 @@
         sigma_re, sigma_im = sigma_in[energy, 0], sigma_in[energy, 1]
         left_re = (matmul(green_re, sigma_re, 0) - matmul(green_im, sigma_im, 0)).astype(jnp.bfloat16)
         left_im = (matmul(green_re, sigma_im, 0) + matmul(green_im, sigma_re, 0)).astype(jnp.bfloat16)
-
-        @pl.when(greater == 0)
-        def _():
-            finish(energy, (left_re, left_im), (green_re, green_im), 1)
-
-        @pl.when(greater == 1)
-        def _():
-            finish(energy, (green_re, green_im), (left_re, left_im), -1)
+        greens.append((green_re, green_im))
+        lefts.append((left_re, left_im))
+
+    @pl.when(greater == 0)
+    def _():
+        for energy in range(energy_dev):
+            finish(energy, lefts[energy], greens[energy], 1)
+
+    @pl.when(greater == 1)
+    def _():
+        for energy in range(energy_dev):
+            finish(energy, greens[energy], lefts[energy], -1)
 
     pl.semaphore_wait(barrier, peer_count - 1)
     for unit in range(base_units + has_spare):
@@ -303,28 +307,30 @@
                 ordered[part, energy] = gathered[unit][part * slot_count + slots[energy]].astype(
                     jnp.float32
                 )
-        for lag in range(slot_count):
+        for block in reversed(range(tile_count)):
+            for lag in range(block * lag_count, (block + 1) * lag_count):
+                for part in range(2):
+                    own_re = ordered[part, lag:, :ROWS]
+                    own_im = ordered[part, lag:, ROWS:]
+                    other_re = ordered[1 - part, : slot_count - lag, :ROWS]
+                    other_im = ordered[1 - part, : slot_count - lag, ROWS:]
+                    sum_re = jnp.sum(own_re * other_re - own_im * other_im, axis=0)
+                    sum_im = jnp.sum(own_re * other_im + own_im * other_re, axis=0)
+                    lagged[unit, part, lag] = jnp.concatenate(
+                        [sum_im * norm_factor, sum_re * -norm_factor]
+                    ).astype(jnp.bfloat16)
             for part in range(2):
-                own_re = ordered[part, lag:, :ROWS]
-                own_im = ordered[part, lag:, ROWS:]
-                other_re = ordered[1 - part, : slot_count - lag, :ROWS]
-                other_im = ordered[1 - part, : slot_count - lag, ROWS:]
-                sum_re = jnp.sum(own_re * other_re - own_im * other_im, axis=0)
-                sum_im = jnp.sum(own_re * other_im + own_im * other_re, axis=0)
-                lagged[unit, part, lag] = jnp.concatenate(
-                    [sum_im * norm_factor, sum_re * -norm_factor]
-                ).astype(jnp.bfloat16)
-        my_unit = firsts[0][0] + unit
-        for i, j in near_owners:
-            pltpu.make_async_remote_copy(
-                src_ref=lagged.at[unit, parts[j], pl.ds(tiles[i] * lag_count, lag_count)],
-                dst_ref=arrived.at[my_unit],
-                send_sem=second_send.at[unit],
-                recv_sem=second_recv.at[unit],
-                device_id=device_of(i, j, 0),
-                device_id_type=pl.DeviceIdType.MESH,
-            ).start()
-        keep_lags(unit).start()
+                copy = pltpu.make_async_remote_copy(
+                    src_ref=lagged.at[unit, part, pl.ds(block * lag_count, lag_count)],
+                    dst_ref=arrived.at[firsts[0][0] + unit],
+                    send_sem=second_send.at[unit],
+                    recv_sem=second_recv.at[unit],
+                    device_id=(momentum * 2 + part, block, rep),
+                    device_id_type=pl.DeviceIdType.MESH,
+                )
+                here = owner == block * 2 + part
+                pl.when(jnp.logical_not(here))(copy.start)
+                pl.when(here)(keep_lags(unit).start)
 
     for unit in range(base_units):
         correlate(unit)

time: 22.5 us -> 23.3 us (1.036)
  Pallas kernels: 22.3 us -> 23.1 us
    pallas_call x1, Pallas kernels: 20.4 us -> 21.2 us  [fused(): pl.pallas_call(functools.partial(polar_kernel, (tile_count, rep_count)),...]
where the time goes in v7:
time: 23.3 us; the launch traced here: 23.2 us
  Pallas kernels  23.1 us (99%)
    pallas_call x1, Pallas kernels, fused(): pl.pallas_call(functools.partial(polar_kernel, (tile_count, rep_count)),...  21.2 us
    pallas_call x1, Pallas kernels, fused(): pl.pallas_call(unpack_kernel, out_shape=jax.ShapeDtypeStruct((1, lag_coun...  1.94 us

profile of v7, /device:TPU:0, one launch (start us, length us, event | category | flops | bytes accessed | tf_op | source)
XLA Modules:
  0.0 23.2 jit_solution(3107612735917771700)
XLA Ops:
  0.0 21.2 %shard_map.37.arrived = bf16[18,4,16,128]{3,2,1,0:T(8,128)(2,1)} custom-call(bf16[2,2,2,192,192]{4,3,2,1,0:T(8,128)(2,1)} %retarded.1, bf16[1,2,2,192,192]{4,3,2,1,0:T(8,128)(2,1)} %self_energy.1, s32[16]{0:T(128)} %energy_of.1), custom_call_target="tpu_custom_call" | custom-call | tf_op jit(solution)/shard_map/pallas_call | solution.py:425
  21.2 1.9 %shard_map.38 = f32[1,4,2,96,192]{4,3,2,1,0:T(8,128)} custom-call(bf16[18,4,16,128]{3,2,1,0:T(8,128)(2,1)} %shard_map.37.arrived), custom_call_target="tpu_custom_call" | custom-call | tf_op jit(solution)/shard_map/pallas_call | solution.py:449

commit v8 on v5

--- a/solution.py
+++ b/solution.py
@@ -249,6 +249,7 @@
     def keep_own(unit):
         gathered[unit][pl.ds(my_slot, energy_dev)] = outgoing[rep, firsts[0][0] + unit]
 
+    greens, lefts = [], []
     for energy in range(energy_dev):
         for load in loads[energy]:
             load.wait()
@@ -256,14 +257,18 @@
         sigma_re, sigma_im = sigma_in[energy, 0], sigma_in[energy, 1]
         left_re = (matmul(green_re, sigma_re, 0) - matmul(green_im, sigma_im, 0)).astype(jnp.bfloat16)
         left_im = (matmul(green_re, sigma_im, 0) + matmul(green_im, sigma_re, 0)).astype(jnp.bfloat16)
-
-        @pl.when(greater == 0)
-        def _():
-            finish(energy, (left_re, left_im), (green_re, green_im), 1)
-
-        @pl.when(greater == 1)
-        def _():
-            finish(energy, (green_re, green_im), (left_re, left_im), -1)
+        greens.append((green_re, green_im))
+        lefts.append((left_re, left_im))
+
+    @pl.when(greater == 0)
+    def _():
+        for energy in range(energy_dev):
+            finish(energy, lefts[energy], greens[energy], 1)
+
+    @pl.when(greater == 1)
+    def _():
+        for energy in range(energy_dev):
+            finish(energy, greens[energy], lefts[energy], -1)
 
     pl.semaphore_wait(barrier, peer_count - 1)
     for unit in range(base_units + has_spare):

time: 22.5 us -> 22.6 us (level)
  no operation moved by 1% of the time
where the time goes in v8:
time: 22.6 us; the launch traced here: 22.4 us
  Pallas kernels  22.4 us (99%)
    pallas_call x1, Pallas kernels, fused(): pl.pallas_call(functools.partial(polar_kernel, (tile_count, rep_count)),...  20.5 us
    pallas_call x1, Pallas kernels, fused(): pl.pallas_call(unpack_kernel, out_shape=jax.ShapeDtypeStruct((1, lag_coun...  1.94 us

profile of v8, /device:TPU:0, one launch (start us, length us, event | category | flops | bytes accessed | tf_op | source)
XLA Modules:
  0.0 22.4 jit_solution(9700324914053603237)
XLA Ops:
  0.0 20.5 %shard_map.37.arrived = bf16[18,4,16,128]{3,2,1,0:T(8,128)(2,1)} custom-call(bf16[2,2,2,192,192]{4,3,2,1,0:T(8,128)(2,1)} %retarded.1, bf16[1,2,2,192,192]{4,3,2,1,0:T(8,128)(2,1)} %self_energy.1, s32[16]{0:T(128)} %energy_of.1), custom_call_target="tpu_custom_call" | custom-call | tf_op jit(solution)/shard_map/pallas_call | solution.py:424
  20.5 1.9 %shard_map.38 = f32[1,4,2,96,192]{4,3,2,1,0:T(8,128)} custom-call(bf16[18,4,16,128]{3,2,1,0:T(8,128)(2,1)} %shard_map.37.arrived), custom_call_target="tpu_custom_call" | custom-call | tf_op jit(solution)/shard_map/pallas_call | solution.py:448

commit v9 on v5

--- a/solution.py
+++ b/solution.py
@@ -266,7 +266,8 @@
             finish(energy, (green_re, green_im), (left_re, left_im), -1)
 
     pl.semaphore_wait(barrier, peer_count - 1)
-    for unit in range(base_units + has_spare):
+    unit_order = [0] + [base_units] * has_spare + list(range(1, base_units))
+    for unit in unit_order:
         send_first(unit)
 
     def wait_for(buffer, sem):
@@ -326,10 +327,11 @@
             ).start()
         keep_lags(unit).start()
 
-    for unit in range(base_units):
-        correlate(unit)
-    if has_spare:
-        pl.when(spares_at[0][0])(functools.partial(correlate, base_units))
+    for unit in unit_order:
+        if unit < base_units:
+            correlate(unit)
+        else:
+            pl.when(spares_at[0][0])(functools.partial(correlate, unit))
 
     for unit in range(base_units):
         wait_for(
@@ -366,20 +368,16 @@
     unit_count, lag_count = arrived.shape[:2]
     row_count = polar.shape[3]
     low_units = row_count // ROWS
-    loads = [
-        pltpu.make_async_copy(arrived.at[:, lag], packed.at[lag], load_sem.at[lag])
-        for lag in range(lag_count)
-    ]
+    load = pltpu.make_async_copy(arrived, packed, load_sem)
     stores = [
         pltpu.make_async_copy(unpacked.at[lag], polar.at[0, lag], store_sem.at[lag])
         for lag in range(lag_count)
     ]
-    for load in loads:
-        load.start()
+    load.start()
+    load.wait()
     for lag in range(lag_count):
-        loads[lag].wait()
         for unit in range(unit_count):
-            values = packed[lag, unit].astype(jnp.float32)
+            values = packed[unit, lag].astype(jnp.float32)
             for part in range(2):
                 block = values[part * ROWS : (part + 1) * ROWS]
                 if unit < low_units:
@@ -446,9 +444,9 @@
         in_specs=[pl.BlockSpec(memory_space=pl.ANY)],
         out_specs=pl.BlockSpec(memory_space=pl.ANY),
         scratch_shapes=[
-            pltpu.VMEM((lag_count, unit_count) + packed, jnp.bfloat16),
+            pltpu.VMEM((unit_count, lag_count) + packed, jnp.bfloat16),
             pltpu.VMEM((lag_count, 2, row_count, block_order), jnp.float32),
-            pltpu.SemaphoreType.DMA((lag_count,)),
+            pltpu.SemaphoreType.DMA,
             pltpu.SemaphoreType.DMA((lag_count,)),
         ],
         compiler_params=pltpu.CompilerParams(vmem_limit_bytes=KERNEL_BYTES),

time: 22.5 us -> 22 us (0.978)
  Pallas kernels: 22.3 us -> 21.8 us
    pallas_call x1, Pallas kernels: 20.4 us -> 19.8 us  [fused(): pl.pallas_call(functools.partial(polar_kernel, (tile_count, rep_count)),...]
where the time goes in v9:
time: 22 us; the launch traced here: 21.8 us
  Pallas kernels  21.8 us (99%)
    pallas_call x1, Pallas kernels, fused(): pl.pallas_call(functools.partial(polar_kernel, (tile_count, rep_count)),...  19.8 us
    pallas_call x1, Pallas kernels, fused(): pl.pallas_call(unpack_kernel, out_shape=jax.ShapeDtypeStruct((1, lag_coun...  1.95 us

profile of v9, /device:TPU:0, one launch (start us, length us, event | category | flops | bytes accessed | tf_op | source)
XLA Modules:
  0.0 21.8 jit_solution(15279560342589579073)
XLA Ops:
  0.0 19.8 %shard_map.37.arrived = bf16[18,4,16,128]{3,2,1,0:T(8,128)(2,1)} custom-call(bf16[2,2,2,192,192]{4,3,2,1,0:T(8,128)(2,1)} %retarded.1, bf16[1,2,2,192,192]{4,3,2,1,0:T(8,128)(2,1)} %self_energy.1, s32[16]{0:T(128)} %energy_of.1), custom_call_target="tpu_custom_call" | custom-call | tf_op jit(solution)/shard_map/pallas_call | solution.py:417
  19.9 1.9 %shard_map.38 = f32[1,4,2,96,192]{4,3,2,1,0:T(8,128)} custom-call(bf16[18,4,16,128]{3,2,1,0:T(8,128)(2,1)} %shard_map.37.arrived), custom_call_target="tpu_custom_call" | custom-call | tf_op jit(solution)/shard_map/pallas_call | solution.py:441

commit v10 on v9

--- a/solution.py
+++ b/solution.py
@@ -253,9 +253,11 @@
         for load in loads[energy]:
             load.wait()
         green_re, green_im = green_in[energy, 0], green_in[energy, 1]
-        sigma_re, sigma_im = sigma_in[energy, 0], sigma_in[energy, 1]
-        left_re = (matmul(green_re, sigma_re, 0) - matmul(green_im, sigma_im, 0)).astype(jnp.bfloat16)
-        left_im = (matmul(green_re, sigma_im, 0) + matmul(green_im, sigma_re, 0)).astype(jnp.bfloat16)
+        both = jnp.concatenate([green_re, green_im])
+        by_re = matmul(both, sigma_in[energy, 0], 0)
+        by_im = matmul(both, sigma_in[energy, 1], 0)
+        left_re = (by_re[:block_order] - by_im[block_order:]).astype(jnp.bfloat16)
+        left_im = (by_im[:block_order] + by_re[block_order:]).astype(jnp.bfloat16)
 
         @pl.when(greater == 0)
         def _():

time: 22 us -> 22 us (level)
  no operation moved by 1% of the time
where the time goes in v10:
time: 22 us; the launch traced here: 21.8 us
  Pallas kernels  21.8 us (99%)
    pallas_call x1, Pallas kernels, fused(): pl.pallas_call(functools.partial(polar_kernel, (tile_count, rep_count)),...  19.9 us
    pallas_call x1, Pallas kernels, fused(): pl.pallas_call(unpack_kernel, out_shape=jax.ShapeDtypeStruct((1, lag_coun...  1.95 us

profile of v10, /device:TPU:0, one launch (start us, length us, event | category | flops | bytes accessed | tf_op | source)
XLA Modules:
  0.0 21.8 jit_solution(9858814514202657191)
XLA Ops:
  0.0 19.9 %shard_map.37.arrived = bf16[18,4,16,128]{3,2,1,0:T(8,128)(2,1)} custom-call(bf16[2,2,2,192,192]{4,3,2,1,0:T(8,128)(2,1)} %retarded.1, bf16[1,2,2,192,192]{4,3,2,1,0:T(8,128)(2,1)} %self_energy.1, s32[16]{0:T(128)} %energy_of.1), custom_call_target="tpu_custom_call" | custom-call | tf_op jit(solution)/shard_map/pallas_call | solution.py:419
  19.9 1.9 %shard_map.38 = f32[1,4,2,96,192]{4,3,2,1,0:T(8,128)} custom-call(bf16[18,4,16,128]{3,2,1,0:T(8,128)(2,1)} %shard_map.37.arrived), custom_call_target="tpu_custom_call" | custom-call | tf_op jit(solution)/shard_map/pallas_call | solution.py:443

commit v11 on v10

--- a/solution.py
+++ b/solution.py
@@ -163,7 +163,6 @@
     firsts = [[first_unit(owners[i][j]) for j in range(2)] for i in range(tile_count)]
     spares_at = [[takes_spare(owners[i][j]) for j in range(2)] for i in range(tile_count)]
     far_first = [(step + half) % tile_count for step in range(tile_count)]
-    near_owners = [(i, j) for i in far_first for j in range(2) if (i, j) != (0, 0)]
     peers = [
         (i, j, k)
         for i in far_first
@@ -306,28 +305,40 @@
                 ordered[part, energy] = gathered[unit][part * slot_count + slots[energy]].astype(
                     jnp.float32
                 )
-        for lag in range(slot_count):
+        def sum_lags(block):
+            for lag in range(block * lag_count, (block + 1) * lag_count):
+                for part in range(2):
+                    own_re = ordered[part, lag:, :ROWS]
+                    own_im = ordered[part, lag:, ROWS:]
+                    other_re = ordered[1 - part, : slot_count - lag, :ROWS]
+                    other_im = ordered[1 - part, : slot_count - lag, ROWS:]
+                    sum_re = jnp.sum(own_re * other_re - own_im * other_im, axis=0)
+                    sum_im = jnp.sum(own_re * other_im + own_im * other_re, axis=0)
+                    lagged[unit, part, lag] = jnp.concatenate(
+                        [sum_im * norm_factor, sum_re * -norm_factor]
+                    ).astype(jnp.bfloat16)
             for part in range(2):
-                own_re = ordered[part, lag:, :ROWS]
-                own_im = ordered[part, lag:, ROWS:]
-                other_re = ordered[1 - part, : slot_count - lag, :ROWS]
-                other_im = ordered[1 - part, : slot_count - lag, ROWS:]
-                sum_re = jnp.sum(own_re * other_re - own_im * other_im, axis=0)
-                sum_im = jnp.sum(own_re * other_im + own_im * other_re, axis=0)
-                lagged[unit, part, lag] = jnp.concatenate(
-                    [sum_im * norm_factor, sum_re * -norm_factor]
-                ).astype(jnp.bfloat16)
-        my_unit = firsts[0][0] + unit
-        for i, j in near_owners:
-            pltpu.make_async_remote_copy(
-                src_ref=lagged.at[unit, parts[j], pl.ds(tiles[i] * lag_count, lag_count)],
-                dst_ref=arrived.at[my_unit],
-                send_sem=second_send.at[unit],
-                recv_sem=second_recv.at[unit],
-                device_id=device_of(i, j, 0),
-                device_id_type=pl.DeviceIdType.MESH,
-            ).start()
-        keep_lags(unit).start()
+                copy = pltpu.make_async_remote_copy(
+                    src_ref=lagged.at[unit, part, pl.ds(block * lag_count, lag_count)],
+                    dst_ref=arrived.at[firsts[0][0] + unit],
+                    send_sem=second_send.at[unit],
+                    recv_sem=second_recv.at[unit],
+                    device_id=(momentum * 2 + part, block, rep),
+                    device_id_type=pl.DeviceIdType.MESH,
+                )
+                here = owner == block * 2 + part
+                pl.when(jnp.logical_not(here))(copy.start)
+                pl.when(here)(keep_lags(unit).start)
+
+        @pl.when(tile < half)
+        def _():
+            for block in reversed(range(tile_count)):
+                sum_lags(block)
+
+        @pl.when(tile >= half)
+        def _():
+            for block in range(tile_count):
+                sum_lags(block)
 
     for unit in unit_order:
         if unit < base_units:

time: 22 us -> 21.7 us (0.986)
    pallas_call x1, Pallas kernels: 19.9 us -> 19.6 us  [fused(): pl.pallas_call(functools.partial(polar_kernel, (tile_count, rep_count)),...]
where the time goes in v11:
time: 21.7 us; the launch traced here: 21.6 us
  Pallas kernels  21.6 us (100%)
    pallas_call x1, Pallas kernels, fused(): pl.pallas_call(functools.partial(polar_kernel, (tile_count, rep_count)),...  19.6 us
    pallas_call x1, Pallas kernels, fused(): pl.pallas_call(unpack_kernel, out_shape=jax.ShapeDtypeStruct((1, lag_coun...  1.95 us

profile of v11, /device:TPU:0, one launch (start us, length us, event | category | flops | bytes accessed | tf_op | source)
XLA Modules:
  0.0 21.6 jit_solution(11774472832805744407)
XLA Ops:
  0.0 19.6 %shard_map.37.arrived = bf16[18,4,16,128]{3,2,1,0:T(8,128)(2,1)} custom-call(bf16[2,2,2,192,192]{4,3,2,1,0:T(8,128)(2,1)} %retarded.1, bf16[1,2,2,192,192]{4,3,2,1,0:T(8,128)(2,1)} %self_energy.1, s32[16]{0:T(128)} %energy_of.1), custom_call_target="tpu_custom_call" | custom-call | tf_op jit(solution)/shard_map/pallas_call | solution.py:430
  19.6 1.9 %shard_map.38 = f32[1,4,2,96,192]{4,3,2,1,0:T(8,128)} custom-call(bf16[18,4,16,128]{3,2,1,0:T(8,128)(2,1)} %shard_map.37.arrived), custom_call_target="tpu_custom_call" | custom-call | tf_op jit(solution)/shard_map/pallas_call | solution.py:454
